TPU v7x, 32 devices: a whole 2x2x4 slice. The times are simulated.
32 devices in a mesh: groups: 2 (over x), lon: 16 (over z, y, core).
Axes of the slice: x: 2, y: 2, z: 4, core: 2. Of those that a mesh axis runs over, the one named last changes fastest.
Arguments:
- fields: bfloat16 [64, 32, 4096], P('groups', 'lon'), parts along dimension 0, may hold values from -6 to 6
- couplings: bfloat16 [32, 9, 64, 64], replicated, may hold values from -0.25 to 0.25
- kappa: float32 [64, 32, 64], P('groups', 'lon'), parts along dimension 0, may hold values from -1 to 1
- coeffs: float32 [3], replicated, may hold values from 0.3 to 1
- foot_lat: int32 [1024, 4], P(('groups', 'lon')), parts along dimension 0, may hold values from 0 to 31
- foot_lon: int32 [1024, 4], P(('groups', 'lon')), parts along dimension 0, may hold values from 0 to 3
- foot_w: bfloat16 [4, 64, 64], replicated, may hold values from -0.375 to 0.375
- thresholds: float32 [16], replicated, may hold values from -2 to 2
- bins: int32 [1024], P(('groups', 'lon')), parts along dimension 0, may hold values from 0 to 15
Outputs:
- filtered: bfloat16 [64, 32, 4096], P('groups', 'lon'), parts along dimension 0
- score: float32 [1024, 64], P(('groups', 'lon')), parts along dimension 0
- summary: float32 [32], P('groups'), parts along dimension 0
There are 2 independent parts, one for each index of `groups`. A program takes and returns all parts, laid end to end along the dimension named above; an argument that names none is the same for every part. Nothing has to cross between parts.
All inputs are finite; a program needn't handle non-finite values.
Results may differ from a plain program's by a relative error of at most 0.014.
Values may be sent and summed in bfloat16 or wider, within the bound.
A program may use at most 128 MiB of HBM per device.

v0:
```python
import jax
import jax.numpy as jnp
from jax import lax
from jax.sharding import PartitionSpec as P

tau_width = 0.5


def padded_2(cells, sides, width):
    for axis, dim in sides:
        count = lax.axis_size(axis)
        head = lax.slice_in_dim(cells, 0, width, axis=dim)
        tail = lax.slice_in_dim(cells, cells.shape[dim] - width, cells.shape[dim], axis=dim)
        cells = jnp.concatenate(
            [
                lax.ppermute(tail, axis, [(i, (i + 1) % count) for i in range(count)]),
                cells,
                lax.ppermute(head, axis, [((i + 1) % count, i) for i in range(count)]),
            ],
            axis=dim,
        )
    return cells


def passed_along(value, axis, steps):
    count = lax.axis_size(axis)
    pairs = [(source, (source + steps) % count) for source in range(count)]
    return lax.ppermute(value, axis, pairs)


def apply_padded(padded, couplings, kappa_mid):
    nlat = padded.shape[0]
    width = padded.shape[1] - 2
    nodes = couplings.shape[-1]
    full = jnp.pad(padded, ((1, 1), (0, 0), (0, 0))).reshape(nlat + 2, width + 2, nodes, -1)
    center = full[1:-1, 1:-1]
    total = kappa_mid[..., None] * center.astype(jnp.float32)
    for row_off in range(3):
        for col_off in range(3):
            piece = full[row_off : row_off + nlat, col_off : col_off + width]
            total = total + jnp.einsum(
                "iab,ijbr->ijar",
                couplings[:, 3 * row_off + col_off],
                piece,
                preferred_element_type=jnp.float32,
            )
    return total


def footprint_terms(source, lat_index, lon_index, keep, foot_w):
    nodes = foot_w.shape[-1]
    picked = source[lat_index, lon_index]
    picked = jnp.where(keep[..., None], picked, jnp.zeros_like(picked))
    picked = picked.reshape(picked.shape[0], picked.shape[1], nodes, -1)
    return jnp.einsum("kab,fkbr->far", foot_w, picked, preferred_element_type=jnp.float32)


def local(fields, couplings, kappa, coeffs, foot_lat, foot_lon, foot_w, thresholds, bins):
    nlat = fields.shape[0]
    local_blocks = fields.shape[1]
    nodes = couplings.shape[-1]
    start = fields.reshape(nlat, local_blocks, nodes, -1).astype(jnp.float32)
    rim_x = padded_2(fields, (("lon", 1),), 1)
    core_one = apply_padded(rim_x, couplings, kappa).astype(jnp.bfloat16)
    term_one = padded_2(core_one.reshape(nlat, local_blocks, -1), (("lon", 1),), 1)
    term_two = 2.0 * apply_padded(term_one, couplings, kappa) - start
    middle = term_one[:, 1:-1].reshape(nlat, local_blocks, nodes, -1).astype(jnp.float32)
    filtered = (coeffs[0] * start + coeffs[1] * middle + coeffs[2] * term_two).astype(jnp.bfloat16)
    filtered = filtered.reshape(nlat, local_blocks, -1)
    eastern = passed_along(filtered, "lon", -1)
    joined = jnp.concatenate([filtered, eastern], axis=1)
    observed = footprint_terms(joined, foot_lat, foot_lon, foot_lon >= 0, foot_w)
    nbins = thresholds.shape[0]
    onehot = (bins[:, None] == jnp.arange(nbins, dtype=jnp.int32)[None, :]).astype(jnp.float32)
    level = jnp.sum(onehot * thresholds[None, :], axis=1)
    ecdf = jnp.mean(jax.nn.sigmoid((level[:, None, None] - observed) / tau_width), axis=2)
    local_totals = jnp.sum(onehot * jnp.sum(ecdf, axis=1)[:, None], axis=0)
    local_counts = jnp.sum(onehot, axis=0) * nodes
    totals, counts = lax.psum((local_totals, local_counts), "lon")
    summary = totals / jnp.maximum(counts, 1.0)
    score = ecdf - jnp.sum(onehot * summary[None, :], axis=1)[:, None]
    return (filtered, score, summary)


def solution(mesh):
    placed = (
        P("groups", "lon", None),
        P(),
        P("groups", "lon", None),
        P(),
        P(("groups", "lon"), None),
        P(("groups", "lon"), None),
        P(),
        P(),
        P(("groups", "lon")),
    )
    return jax.shard_map(
        local,
        mesh=mesh,
        in_specs=placed,
        out_specs=(P("groups", "lon", None), P(("groups", "lon"), None), P("groups")),
        check_vma=False,
    )
```

profile of v0, /device:TPU:0, one launch (start us, length us, event | category | flops | bytes accessed | tf_op | source)
XLA Modules:
  0.0 148.2 jit_solution(303393813121165065)
XLA Ops:
  0.7 2.4 %fusion.110 = (bf16[32,1,4096]{2,1,0:T(2,128)(2,1)S(1)}, bf16[32,1,4096]{2,1,0:T(2,128)(2,1)S(1)}) fusion(bf16[32,2,4096]{2,1,0:T(2,128)(2,1)} %param.9), kind=kLoop, calls=%fused_computation.132 | loop fusion | bytes 1048576 | tf_op jit(solution)/shard_map/slice | solution.py:13
  3.6 5.1 %collective-permute-start.1 = (bf16[32,1,4096]{2,1,0:T(2,128)(2,1)S(1)}, bf16[32,1,4096]{2,1,0:T(2,128)(2,1)S(1)}, u32[]{:S(2)}, u32[]{:S(2)}) collective-permute-start(bf16[32,1,4096]{2,1,0:T(2,128)(2,1)S(1)} %get-tuple-element.25), channel_id=1, source_target_pairs={{1,0},{2,1},{3,2},{4,3},{5,4},{6,5},{7,6},{8,7},{9,8},{10,9},{11,1... | collective-permute-start | bytes 786440 | tf_op jit(solution)/shard_map/ppermute | solution.py:18
  8.6 6.9 %collective-permute-done = bf16[32,1,4096]{2,1,0:T(2,128)(2,1)S(1)} collective-permute-done((bf16[32,1,4096]{2,1,0:T(2,128)(2,1)S(1)}, bf16[32,1,4096]{2,1,0:T(2,128)(2,1)S(1)}, u32[]{:S(2)}, u32[]{:S(2)}) %collective-permute-start) | collective-permute-done | bytes 262176 | tf_op jit(solution)/shard_map/ppermute | solution.py:16
  15.6 2.6 %select_maximum_fusion = bf16[34,4,4096]{2,1,0:T(4,128)(2,1)} fusion(bf16[32,1,4096]{2,1,0:T(2,128)(2,1)S(1)} %collective-permute-done.1, bf16[32,2,4096]{2,1,0:T(2,128)(2,1)S(1)} %copy-done.1, bf16[32,1,4096]{2,1,0:T(2,128)(2,1)S(1)} %collective-permute-done), kind=kLoop, calls=%fused_computation.45 | loop fusion | flops 6684672 | bytes 2162688 | tf_op jit(solution)/shard_map/concatenate | solution.py:14
  18.2 3.5 %reshape.31 = bf16[34,4,64,64]{3,2,1,0:T(8,128)(2,1)S(1)} reshape(bf16[34,4,4096]{2,1,0:T(4,128)(2,1)} %select_maximum_fusion) | data formatting | bytes 2228224 | tf_op jit(solution)/shard_map/reshape | solution.py:35
  21.8 3.0 %fusion.81 = f32[32,2,64,64]{3,2,1,0:T(8,128)} fusion(bf16[34,4,64,64]{3,2,1,0:T(8,128)(2,1)S(1)} %reshape.31, bf16[32,9,64,64]{3,2,1,0:T(8,128)(2,1)} %param.10), kind=kOutput, calls=%fused_computation.91 | convolution fusion | flops 33554432 | bytes 2686976 | tf_op jit(solution)/shard_map/iab,ijbr->ijar/dot_general | solution.py:41
  24.8 1.8 %fusion.59 = f32[32,2,64,64]{3,2,1,0:T(8,128)} fusion(bf16[34,4,64,64]{3,2,1,0:T(8,128)(2,1)S(1)} %reshape.31, bf16[32,9,64,64]{3,2,1,0:T(8,128)(2,1)S(1)} %bitcast.212), kind=kOutput, calls=%fused_computation.69 | convolution fusion | flops 33554432 | bytes 3801088 | tf_op jit(solution)/shard_map/iab,ijbr->ijar/dot_general | solution.py:41
  26.6 1.8 %fusion.62 = f32[32,2,64,64]{3,2,1,0:T(8,128)} fusion(bf16[34,4,64,64]{3,2,1,0:T(8,128)(2,1)S(1)} %reshape.31, bf16[32,9,64,64]{3,2,1,0:T(8,128)(2,1)S(1)} %bitcast.212), kind=kOutput, calls=%fused_computation.72 | convolution fusion | flops 33554432 | bytes 3801088 | tf_op jit(solution)/shard_map/iab,ijbr->ijar/dot_general | solution.py:41
  28.4 1.8 %fusion.65 = f32[32,2,64,64]{3,2,1,0:T(8,128)} fusion(bf16[34,4,64,64]{3,2,1,0:T(8,128)(2,1)S(1)} %reshape.31, bf16[32,9,64,64]{3,2,1,0:T(8,128)(2,1)S(1)} %bitcast.212), kind=kOutput, calls=%fused_computation.75 | convolution fusion | flops 33554432 | bytes 3801088 | tf_op jit(solution)/shard_map/iab,ijbr->ijar/dot_general | solution.py:41
  30.2 1.8 %fusion.69 = f32[32,2,64,64]{3,2,1,0:T(8,128)} fusion(bf16[34,4,64,64]{3,2,1,0:T(8,128)(2,1)S(1)} %reshape.31, bf16[32,9,64,64]{3,2,1,0:T(8,128)(2,1)S(1)} %bitcast.212), kind=kOutput, calls=%fused_computation.79 | convolution fusion | flops 33554432 | bytes 3801088 | tf_op jit(solution)/shard_map/iab,ijbr->ijar/dot_general | solution.py:41
  32.0 1.9 %fusion.72 = f32[32,2,64,64]{3,2,1,0:T(8,128)} fusion(bf16[34,4,64,64]{3,2,1,0:T(8,128)(2,1)S(1)} %reshape.31, bf16[32,9,64,64]{3,2,1,0:T(8,128)(2,1)S(1)} %bitcast.212), kind=kOutput, calls=%fused_computation.82 | convolution fusion | flops 33554432 | bytes 3801088 | tf_op jit(solution)/shard_map/iab,ijbr->ijar/dot_general | solution.py:41
  33.9 1.8 %fusion.75 = f32[32,2,64,64]{3,2,1,0:T(8,128)} fusion(bf16[34,4,64,64]{3,2,1,0:T(8,128)(2,1)S(1)} %reshape.31, bf16[32,9,64,64]{3,2,1,0:T(8,128)(2,1)S(1)} %bitcast.212), kind=kOutput, calls=%fused_computation.85 | convolution fusion | flops 33554432 | bytes 3801088 | tf_op jit(solution)/shard_map/iab,ijbr->ijar/dot_general | solution.py:41
  35.7 1.8 %fusion.78 = f32[32,2,64,64]{3,2,1,0:T(8,128)} fusion(bf16[34,4,64,64]{3,2,1,0:T(8,128)(2,1)S(1)} %reshape.31, bf16[32,9,64,64]{3,2,1,0:T(8,128)(2,1)S(1)} %bitcast.212), kind=kOutput, calls=%fused_computation.88 | convolution fusion | flops 33554432 | bytes 3801088 | tf_op jit(solution)/shard_map/iab,ijbr->ijar/dot_general | solution.py:41
  38.8 7.3 %fusion.7 = bf16[32,2,64,64]{2,3,1,0:T(8,128)(2,1)S(1)} fusion(f32[32,2,64,64]{3,2,1,0:T(8,128)} %fusion.59, f32[32,2,64,64]{3,2,1,0:T(8,128)} %fusion.62, f32[32,2,64,64]{3,2,1,0:T(8,128)} %fusion.65, f32[32,2,64,64]{3,2,1,0:T(8,128)} %fusion.69, f32[32,2,64,64]{3,2,1,0:T(8,128)} %fusion.72, f32[32,2,64,64]{3,2,1,0:T(8,128)} %fusion.75, ...), kind=kOutput, calls=%fused_computation.22 | convolution fusion | flops 36700160 | bytes 20004864 | tf_op jit(solution)/shard_map/iab,ijbr->ijar/dot_general | solution.py:41
  48.6 4.9 %collective-permute-start.2 = (bf16[32,1,4096]{2,0,1:T(8,128)(2,1)}, bf16[32,1,4096]{2,0,1:T(8,128)(2,1)S(1)}, u32[]{:S(2)}, u32[]{:S(2)}) collective-permute-start(bf16[32,1,4096]{2,0,1:T(8,128)(2,1)} %get-tuple-element.22), channel_id=1, source_target_pairs={{0,1},{1,2},{2,3},{3,4},{4,5},{5,6},{6,7},{7,8},{8,9},{9,10},{10,1... | collective-permute-start | bytes 786440 | tf_op jit(solution)/shard_map/ppermute | solution.py:16
  53.5 2.2 %reshape.66 = f32[32,2,64,64]{3,2,1,0:T(8,128)S(1)} reshape(bf16[32,2,4096]{2,1,0:T(2,128)(2,1)} %param.9) | data formatting | bytes 1572864 | tf_op jit(solution)/shard_map/convert_element_type | solution.py:62
  55.7 1.8 %copy.64 = f32[32,2,64,64]{2,3,1,0:T(8,128)} copy(f32[32,2,64,64]{3,2,1,0:T(8,128)S(1)} %reshape.66) | data formatting | bytes 2097152 | tf_op jit(solution)/shard_map/convert_element_type | solution.py:62
  58.2 2.6 %fusion.33 = bf16[34,4,4096]{2,0,1:T(8,128)(2,1)} fusion(bf16[32,1,4096]{2,0,1:T(8,128)(2,1)} %collective-permute-done.3, bf16[32,2,4096]{2,0,1:T(8,128)(2,1)} %copy-done.3, bf16[32,1,4096]{2,0,1:T(8,128)(2,1)S(1)} %collective-permute-done.2), kind=kLoop, calls=%fused_computation.44 | loop fusion | flops 6684672 | bytes 2162688 | tf_op jit(solution)/shard_map/concatenate | solution.py:14
  60.8 3.3 %reshape.67 = bf16[34,4,64,64]{3,2,0,1:T(8,128)(2,1)S(1)} reshape(bf16[34,4,4096]{2,0,1:T(8,128)(2,1)} %fusion.33) | data formatting | bytes 2228224 | tf_op jit(solution)/shard_map/reshape | solution.py:35
  64.0 4.1 %fusion.108 = (bf16[32,2,64,64]{3,2,0,1:T(8,128)(2,1)}, bf16[32,2,64,64]{3,2,0,1:T(8,128)(2,1)}, bf16[32,2,64,64]{3,2,0,1:T(8,128)(2,1)}, bf16[32,2,64,64]{3,2,0...) fusion(bf16[34,4,64,64]{3,2,0,1:T(8,128)(2,1)S(1)} %reshape.67), kind=kLoop, calls=%fused_computation.130 | loop fusion | bytes 9437184 | tf_op jit(solution)/shard_map/slice | solution.py:40
  68.1 1.6 %copy.136 = bf16[32,2,64,64]{2,3,1,0:T(8,128)(2,1)S(1)} copy(bf16[32,2,64,64]{3,2,0,1:T(8,128)(2,1)} %get-tuple-element.21) | data formatting | bytes 1048576
  73.0 1.6 %fusion.51 = f32[32,2,64,64]{3,2,1,0:T(8,128)S(1)} fusion(bf16[32,2,64,64]{3,2,0,1:T(8,128)(2,1)S(1)} %copy-done.9, bf16[32,9,64,64]{3,2,1,0:T(8,128)(2,1)} %param.10), kind=kOutput, calls=%fused_computation.61 | convolution fusion | flops 33554432 | bytes 2097152 | tf_op jit(solution)/shard_map/iab,ijbr->ijar/dot_general | solution.py:41
  74.6 1.6 %fusion.49 = f32[32,2,64,64]{3,2,1,0:T(8,128)S(1)} fusion(bf16[32,2,64,64]{3,2,0,1:T(8,128)(2,1)S(1)} %copy-done.8, bf16[32,9,64,64]{3,2,1,0:T(8,128)(2,1)} %param.10), kind=kOutput, calls=%fused_computation.59 | convolution fusion | flops 33554432 | bytes 2097152 | tf_op jit(solution)/shard_map/iab,ijbr->ijar/dot_general | solution.py:41
  81.2 1.7 %fusion.41 = f32[32,2,64,64]{3,2,1,0:T(8,128)S(1)} fusion(bf16[32,2,64,64]{3,2,0,1:T(8,128)(2,1)S(1)} %copy-done.4, bf16[32,9,64,64]{3,2,1,0:T(8,128)(2,1)} %param.10), kind=kOutput, calls=%fused_computation.51 | convolution fusion | flops 33554432 | bytes 2097152 | tf_op jit(solution)/shard_map/iab,ijbr->ijar/dot_general | solution.py:41
  83.1 4.7 %fusion.6 = bf16[32,2,64,64]{2,3,1,0:T(8,128)(2,1)S(1)} fusion(f32[32,2,64,64]{2,3,1,0:T(8,128)S(1)} %copy-done.2, f32[32,2,64,64]{3,2,1,0:T(8,128)S(1)} %fusion.41, f32[32,2,64,64]{3,2,1,0:T(8,128)S(1)} %fusion.43, f32[32,2,64,64]{3,2,1,0:T(8,128)S(1)} %fusion.45, f32[32,2,64,64]{3,2,1,0:T(8,128)S(1)} %fusion.67, f32[32,2,64,64]{3,2,1,0:T(8,128)S(1)} %fusion.47, ...), kind=kOutput, calls=%fused_computation.12 | convolution fusion | flops 38797312 | bytes 12076544 | tf_op jit(solution)/shard_map/iab,ijbr->ijar/dot_general | solution.py:41
  89.3 4.5 %collective-permute-start.4 = (bf16[32,2,4096]{2,1,0:T(2,128)(2,1)S(1)}, bf16[32,2,4096]{2,1,0:T(2,128)(2,1)S(1)}, u32[]{:S(2)}, u32[]{:S(2)}) collective-permute-start(bf16[32,2,4096]{2,1,0:T(2,128)(2,1)S(1)} %reshape.68), channel_id=1, source_target_pairs={{0,15},{1,0},{2,1},{3,2},{4,3},{5,4},{6,5},{7,6},{8,7},{9,8},{10,9... | collective-permute-start | bytes 1572872 | tf_op jit(solution)/shard_map/ppermute | solution.py:28
  94.2 6.3 %collective-permute-done.4 = bf16[32,2,4096]{2,1,0:T(2,128)(2,1)S(1)} collective-permute-done((bf16[32,2,4096]{2,1,0:T(2,128)(2,1)S(1)}, bf16[32,2,4096]{2,1,0:T(2,128)(2,1)S(1)}, u32[]{:S(2)}, u32[]{:S(2)}) %collective-permute-start.4) | collective-permute-done | bytes 524320 | tf_op jit(solution)/shard_map/ppermute | solution.py:28
  101.6 3.9 %gather_fusion = bf16[128,4096]{1,0:T(8,128)(2,1)S(1)} fusion(bf16[32,4,4096]{2,1,0:T(4,128)(2,1)S(1)} %pad_maximum_fusion, s32[128]{0:T(128)S(1)} %reshape.36), kind=kCustom, calls=%fused_computation | custom fusion | bytes 2098176 | tf_op jit(solution)/shard_map/gather | solution.py:52
  105.4 2.3 %gather.6 = bf16[32,4,64,64]{3,2,1,0:T(8,128)(2,1)S(1)} reshape(bf16[128,4096]{1,0:T(8,128)(2,1)S(1)} %gather_fusion) | data formatting | bytes 2097152 | tf_op jit(solution)/shard_map/gather | solution.py:52
  107.7 2.9 %copy.100 = bf16[32,4,64,64]{2,3,1,0:T(8,128)(2,1)} copy(bf16[32,4,64,64]{3,2,1,0:T(8,128)(2,1)S(1)} %gather.6) | data formatting | bytes 2097152 | tf_op jit(solution)/shard_map/gather | solution.py:52
  110.6 2.4 %fusion.37 = f32[32,64]{1,0:T(8,128)S(1)} fusion(bf16[32,4,64,64]{2,3,1,0:T(8,128)(2,1)} %copy.100, pred[32,4]{1,0:T(8,128)(4,1)S(1)} %copy.96, f32[32]{0:T(128)S(1)} %select_reduce_fusion.2, bf16[4,64,64]{2,1,0:T(8,128)(2,1)S(1)} %copy-done), kind=kOutput, calls=%fused_computation.48 | convolution fusion | flops 68417536 | bytes 1089792 | tf_op jit(solution)/shard_map/kab,fkbr->far/dot_general | solution.py:55
  113.3 34.1 %all-reduce.2 = (f32[16]{0:T(128)S(1)}, f32[16]{0:T(128)S(1)}) all-reduce(f32[16]{0:T(128)S(1)} %get-tuple-element.10, f32[16]{0:T(128)S(1)} %broadcast_multiply_fusion), channel_id=1, replica_groups=mesh['groups'=2,'lon'=16] {'lon'}, use_global_device_ids=true, to_apply=%region_4.5 | all-reduce | flops 32 | bytes 256 | tf_op jit(solution)/shard_map/psum | solution.py:79
  (76 shorter events, 17.3 us)
Async XLA Ops:
  0.6 110.0 %copy-start = (bf16[4,64,64]{2,1,0:T(8,128)(2,1)S(1)}, bf16[4,64,64]{2,1,0:T(8,128)(2,1)}, u32[]{:S(2)}) copy-start(bf16[4,64,64]{2,1,0:T(8,128)(2,1)} %param.15) | copy-start | bytes 98308
  0.6 14.9 %copy-start.1 = (bf16[32,2,4096]{2,1,0:T(2,128)(2,1)S(1)}, bf16[32,2,4096]{2,1,0:T(2,128)(2,1)}, u32[]{:S(2)}) copy-start(bf16[32,2,4096]{2,1,0:T(2,128)(2,1)} %param.9) | copy-start | bytes 1572868
  3.1 12.5 %collective-permute-start = (bf16[32,1,4096]{2,1,0:T(2,128)(2,1)S(1)}, bf16[32,1,4096]{2,1,0:T(2,128)(2,1)S(1)}, u32[]{:S(2)}, u32[]{:S(2)}) collective-permute-start(bf16[32,1,4096]{2,1,0:T(2,128)(2,1)S(1)} %get-tuple-element.24), channel_id=1, source_target_pairs={{0,1},{1,2},{2,3},{3,4},{4,5},{5,6},{6,7},{7,8},{8,9},{9,10},{10,1... | collective-permute-start | bytes 786440 | tf_op jit(solution)/shard_map/ppermute | solution.py:16
  3.6 12.0 %collective-permute-start.1 = (bf16[32,1,4096]{2,1,0:T(2,128)(2,1)S(1)}, bf16[32,1,4096]{2,1,0:T(2,128)(2,1)S(1)}, u32[]{:S(2)}, u32[]{:S(2)}) collective-permute-start(bf16[32,1,4096]{2,1,0:T(2,128)(2,1)S(1)} %get-tuple-element.25), channel_id=1, source_target_pairs={{1,0},{2,1},{3,2},{4,3},{5,4},{6,5},{7,6},{8,7},{9,8},{10,9},{11,1... | collective-permute-start | bytes 786440 | tf_op jit(solution)/shard_map/ppermute | solution.py:18
  21.7 3.1 %slice-start = ((s8[4718592]{0:T(1024)(128)(4,1)}), s8[4194304]{0:T(1024)(128)(4,1)S(1)}, s32[]{:S(2)}) async-start(s8[4718592]{0:T(1024)(128)(4,1)} %bitcast.211), calls=%async_computation | async-start | bytes 8388608
  21.8 3.0 %slice-start.1 = ((s8[4718592]{0:T(1024)(128)(4,1)}), s8[524288]{0:T(1024)(128)(4,1)S(1)}, s32[]{:S(2)}) async-start(s8[4718592]{0:T(1024)(128)(4,1)} %bitcast.211), calls=%async_computation.1 | async-start | bytes 1048576
  37.5 1.3 copy-start.13
  47.6 5.8 %copy-start.3 = (bf16[32,2,4096]{2,0,1:T(8,128)(2,1)}, bf16[32,2,4096]{2,0,1:T(8,128)(2,1)S(1)}, u32[]{:S(2)}) copy-start(bf16[32,2,4096]{2,0,1:T(8,128)(2,1)S(1)} %reshape.32) | copy-start | bytes 1572868
  48.6 9.6 %collective-permute-start.2 = (bf16[32,1,4096]{2,0,1:T(8,128)(2,1)}, bf16[32,1,4096]{2,0,1:T(8,128)(2,1)S(1)}, u32[]{:S(2)}, u32[]{:S(2)}) collective-permute-start(bf16[32,1,4096]{2,0,1:T(8,128)(2,1)} %get-tuple-element.22), channel_id=1, source_target_pairs={{0,1},{1,2},{2,3},{3,4},{4,5},{5,6},{6,7},{7,8},{8,9},{9,10},{10,1... | collective-permute-start | bytes 786440 | tf_op jit(solution)/shard_map/ppermute | solution.py:16
  53.5 4.7 %collective-permute-start.3 = (bf16[32,1,4096]{2,0,1:T(8,128)(2,1)}, bf16[32,1,4096]{2,0,1:T(8,128)(2,1)}, u32[]{:S(2)}, u32[]{:S(2)}) collective-permute-start(bf16[32,1,4096]{2,0,1:T(8,128)(2,1)} %get-tuple-element.23), channel_id=1, source_target_pairs={{1,0},{2,1},{3,2},{4,3},{5,4},{6,5},{7,6},{8,7},{9,8},{10,9},{11,1... | collective-permute-start | bytes 786440 | tf_op jit(solution)/shard_map/ppermute | solution.py:18
  55.6 1.9 %copy-start.15 = (f32[3]{0:T(128)S(1)}, f32[3]{0:T(128)}, u32[]{:S(2)}) copy-start(f32[3]{0:T(128)} %param.12) | copy-start | bytes 40
  69.7 1.6 %copy-start.10 = (bf16[32,2,64,64]{3,2,0,1:T(8,128)(2,1)S(1)}, bf16[32,2,64,64]{3,2,0,1:T(8,128)(2,1)}, u32[]{:S(2)}) copy-start(bf16[32,2,64,64]{3,2,0,1:T(8,128)(2,1)} %get-tuple-element.20) | copy-start | bytes 1572868
  71.3 1.6 %copy-start.9 = (bf16[32,2,64,64]{3,2,0,1:T(8,128)(2,1)S(1)}, bf16[32,2,64,64]{3,2,0,1:T(8,128)(2,1)}, u32[]{:S(2)}) copy-start(bf16[32,2,64,64]{3,2,0,1:T(8,128)(2,1)} %get-tuple-element.19) | copy-start | bytes 1572868
  73.0 1.6 %copy-start.8 = (bf16[32,2,64,64]{3,2,0,1:T(8,128)(2,1)S(1)}, bf16[32,2,64,64]{3,2,0,1:T(8,128)(2,1)}, u32[]{:S(2)}) copy-start(bf16[32,2,64,64]{3,2,0,1:T(8,128)(2,1)} %get-tuple-element.18) | copy-start | bytes 1572868
  74.6 1.6 %copy-start.7 = (bf16[32,2,64,64]{3,2,0,1:T(8,128)(2,1)S(1)}, bf16[32,2,64,64]{3,2,0,1:T(8,128)(2,1)}, u32[]{:S(2)}) copy-start(bf16[32,2,64,64]{3,2,0,1:T(8,128)(2,1)} %get-tuple-element.17) | copy-start | bytes 1572868
  76.2 1.6 %copy-start.6 = (bf16[32,2,64,64]{3,2,0,1:T(8,128)(2,1)S(1)}, bf16[32,2,64,64]{3,2,0,1:T(8,128)(2,1)}, u32[]{:S(2)}) copy-start(bf16[32,2,64,64]{3,2,0,1:T(8,128)(2,1)} %get-tuple-element.16) | copy-start | bytes 1572868
  77.9 1.6 %copy-start.5 = (bf16[32,2,64,64]{3,2,0,1:T(8,128)(2,1)S(1)}, bf16[32,2,64,64]{3,2,0,1:T(8,128)(2,1)}, u32[]{:S(2)}) copy-start(bf16[32,2,64,64]{3,2,0,1:T(8,128)(2,1)} %get-tuple-element.15) | copy-start | bytes 1572868
  79.5 1.7 %copy-start.4 = (bf16[32,2,64,64]{3,2,0,1:T(8,128)(2,1)S(1)}, bf16[32,2,64,64]{3,2,0,1:T(8,128)(2,1)}, u32[]{:S(2)}) copy-start(bf16[32,2,64,64]{3,2,0,1:T(8,128)(2,1)} %get-tuple-element.14) | copy-start | bytes 1572868
  81.1 1.8 %copy-start.2 = (f32[32,2,64,64]{2,3,1,0:T(8,128)S(1)}, f32[32,2,64,64]{2,3,1,0:T(8,128)}, u32[]{:S(2)}) copy-start(f32[32,2,64,64]{2,3,1,0:T(8,128)} %copy.64) | copy-start | bytes 3145732
  81.1 2.0 %copy-start.11 = (bf16[32,2,64,64]{3,2,0,1:T(8,128)(2,1)S(1)}, bf16[32,2,64,64]{3,2,0,1:T(8,128)(2,1)}, u32[]{:S(2)}) copy-start(bf16[32,2,64,64]{3,2,0,1:T(8,128)(2,1)} %get-tuple-element.13) | copy-start | bytes 1572868
  87.8 5.9 %copy-start.14 = (s32[32,4]{0,1:T(4,128)S(1)}, s32[32,4]{0,1:T(4,128)}, u32[]{:S(2)}) copy-start(s32[32,4]{0,1:T(4,128)} %param.14) | copy-start | bytes 1540
  87.8 6.0 %copy-start.16 = (s32[32,4]{0,1:T(4,128)S(1)}, s32[32,4]{0,1:T(4,128)}, u32[]{:S(2)}) copy-start(s32[32,4]{0,1:T(4,128)} %param.13) | copy-start | bytes 1540
  87.8 6.2 %copy-start.17 = (s32[32]{0:T(128)S(1)}, s32[32]{0:T(128)}, u32[]{:S(2)}) copy-start(s32[32]{0:T(128)} %param.17) | copy-start | bytes 388
  87.9 6.2 %copy-start.18 = (f32[16]{0:T(128)S(1)}, f32[16]{0:T(128)}, u32[]{:S(2)}) copy-start(f32[16]{0:T(128)} %param.16) | copy-start | bytes 196
  89.3 12.3 %copy-start.12 = (bf16[32,2,4096]{2,1,0:T(2,128)(2,1)}, bf16[32,2,4096]{2,1,0:T(2,128)(2,1)S(1)}, u32[]{:S(2)}) copy-start(bf16[32,2,4096]{2,1,0:T(2,128)(2,1)S(1)} %reshape.68) | copy-start | bytes 1572868
  89.3 11.2 %collective-permute-start.4 = (bf16[32,2,4096]{2,1,0:T(2,128)(2,1)S(1)}, bf16[32,2,4096]{2,1,0:T(2,128)(2,1)S(1)}, u32[]{:S(2)}, u32[]{:S(2)}) collective-permute-start(bf16[32,2,4096]{2,1,0:T(2,128)(2,1)S(1)} %reshape.68), channel_id=1, source_target_pairs={{0,15},{1,0},{2,1},{3,2},{4,3},{5,4},{6,5},{7,6},{8,7},{9,8},{10,9... | collective-permute-start | bytes 1572872 | tf_op jit(solution)/shard_map/ppermute | solution.py:28
  147.4 0.8 copy-start.19
where the time goes:
time: 149 us; the launch traced here: 148 us
  matrix products  43.1 us (29%)
  local copies, waits for them, and re-layouts  34.5 us (23%)
  blocking collectives  34.1 us (23%)
  starting transfers between devices  14.9 us (10%)
  waiting for transfers between devices  13.2 us (9%)
  other arithmetic  7.4 us (5%)
    dot_general x18, matrix products, apply_padded(): jnp.einsum('iab,ijbr->ijar', couplings[:, 3 * row_off + col_off], piece,...  40.6 us
    psum x1, blocking collectives, local(): totals, counts = lax.psum((local_totals, local_counts), 'lon')  34.1 us
    gather x3, local copies, waits for them, and re-layouts, footprint_terms(): picked = source[lat_index, lon_index]  9.03 us
    ppermute x2, waiting for transfers between devices, padded_2(): lax.ppermute(tail, axis, [(i, (i + 1) % count) for i in range(count)])  6.91 us
    reshape x2, local copies, waits for them, and re-layouts, apply_padded(): jnp.pad(padded, ((1, 1), (0, 0), (0, 0)))  6.75 us
    ppermute x1, waiting for transfers between devices, passed_along(): return lax.ppermute(value, axis, pairs)  6.27 us
    ppermute x2, starting transfers between devices, padded_2(): lax.ppermute(tail, axis, [(i, (i + 1) % count) for i in range(count)])  5.39 us
    concatenate x2, other arithmetic, padded_2(): jnp.concatenate([lax.ppermute(tail, axis, [(i, (i + 1) % count) for i in...  5.2 us
  transfers between devices with their start and end apart: 5, of which 2 were waited for; matrix products, arithmetic and copies ran while one was open for 3% of the time, Pallas kernels for 0%

commit v1 on v0

v1 whole, which is shorter than its diff:
```python
import functools

import jax
import jax.numpy as jnp
from jax import lax
from jax.experimental import pallas as pl
from jax.experimental.pallas import tpu as pltpu
from jax.sharding import PartitionSpec as P

MESH = pl.DeviceIdType.MESH
F32 = jnp.float32
BF16 = jnp.bfloat16
tau_width = 0.5
LANES = 128


def kernel(n, nlat, nb, nobs, nk, nbins, nch, *refs):
    (x_ref, kt_ref, coup_hbm, foot_w_ref, binscol_ref, coef_ref, lat_ref, lon_ref, thr_ref, bins_ref,
     filt_ref, score_ref, summ_ref,
     xw, xo, xe, kw, ke, coup, wc, kx, t1, feast, fb, ecdf, msg, inbox,
     xs_sem, xr_sem, ks_sem, kr_sem, c_sem, fs_sem, fr_sem, ms_sem, mr_sem) = refs
    me = lax.axis_index("lon")
    east, west = lax.rem(me + 1, n), lax.rem(me + n - 1, n)
    ch = nlat // nch
    w2 = 2 * nb

    barrier = pltpu.get_barrier_semaphore()

    def greet(off, carry):
        pl.semaphore_signal(barrier, inc=1, device_id={"lon": lax.rem(me + off, n)}, device_id_type=MESH)
        return carry

    lax.fori_loop(1, n, greet, 0)
    c_copy = pltpu.make_async_copy(coup_hbm, coup, c_sem)
    c_copy.start()
    pl.semaphore_wait(barrier, n - 1)

    kcopies = []
    for side, (dst, dev) in enumerate(((kw, east), (ke, west))):
        cp = pltpu.make_async_remote_copy(
            src_ref=kt_ref, dst_ref=dst, send_sem=ks_sem.at[side], recv_sem=kr_sem.at[side],
            device_id={"lon": dev}, device_id_type=MESH)
        cp.start()
        kcopies.append(cp)
    xcopies = []
    for c in range(nch):
        pair = []
        for side, (dst, dev) in enumerate(((xw, east), (xe, west))):
            cp = pltpu.make_async_remote_copy(
                src_ref=x_ref.at[pl.ds(c * ch, ch)], dst_ref=dst.at[pl.ds(1 + c * ch, ch)],
                send_sem=xs_sem.at[side, c], recv_sem=xr_sem.at[side, c],
                device_id={"lon": dev}, device_id_type=MESH)
            cp.start()
            pair.append(cp)
        xcopies.append(pair)

    zero = jnp.zeros((nb, w2), BF16)
    for buf in (xw, xo, xe):
        buf[0] = zero
        buf[nlat + 1] = zero
    t1[0] = jnp.zeros((nb, 2 * w2), BF16)
    t1[nlat + 1] = jnp.zeros((nb, 2 * w2), BF16)
    xo[pl.ds(1, nlat)] = x_ref[...]

    c_copy.wait()

    def widen(i, carry):
        wc[i] = jnp.concatenate(
            [coup[i, pl.ds(3 * a, 3)].reshape(3 * nb, nb) for a in range(3)], axis=1)
        return carry

    lax.fori_loop(0, nlat, widen, 0, unroll=2)

    for cp in kcopies:
        cp.wait()
    kwv, kov, kev = kw[...], kt_ref[...], ke[...]
    low = lax.broadcasted_iota(jnp.int32, (nb, w2), 1) < nb

    def spread(v, j):
        return jnp.broadcast_to(v[:, j:j + 1], (nb, w2))

    for i in range(nlat):
        kx[i, :, 0:w2] = spread(kwv, 2 * i + 1)
        kx[i, :, w2:2 * w2] = jnp.where(low, spread(kov, 2 * i), spread(kov, 2 * i + 1))
        kx[i, :, 2 * w2:3 * w2] = spread(kev, 2 * i)

    c0, c1, c2 = coef_ref[0], coef_ref[1], coef_ref[2]

    def first(i, carry):
        rhs = jnp.concatenate(
            [buf[pl.ds(i, 3)].reshape(3 * nb, w2) for buf in (xw, xo, xe)], axis=1)
        p = jnp.dot(wc[i], rhs, preferred_element_type=F32)
        centre = jnp.concatenate([buf[i + 1].astype(F32) for buf in (xw, xo, xe)], axis=1)
        mid = p[nb:2 * nb] + kx[i] * centre
        total = p[0:nb, 0:2 * w2] + p[2 * nb:3 * nb, w2:3 * w2] + mid[:, nb:nb + 2 * w2]
        t1[i + 1] = total.astype(BF16)
        return carry

    def second(i, carry):
        p = jnp.dot(wc[i], t1[pl.ds(i, 3)].reshape(3 * nb, 2 * w2), preferred_element_type=F32)
        own = t1[i + 1].astype(F32)[:, nb:nb + w2]
        st = (p[0:nb, 0:w2] + p[2 * nb:3 * nb, w2:2 * w2] + p[nb:2 * nb, nb:nb + w2]
              + kx[i, :, w2:2 * w2] * own)
        x = x_ref[i].astype(F32)
        f = (c0 * x + c1 * own + c2 * (2.0 * st - x)).astype(BF16)
        filt_ref[i] = f
        fb[2 * i] = f[:, 0:nb]
        fb[2 * i + 1] = f[:, nb:w2]
        return carry

    fcopies = []
    for c in range(nch):
        for cp in xcopies[c]:
            cp.wait_recv()
        last = c == nch - 1
        t_lo, t_hi = max(c * ch - 1, 0), nlat if last else (c + 1) * ch - 1
        f_lo, f_hi = max(c * ch - 2, 0), nlat if last else (c + 1) * ch - 2
        lax.fori_loop(t_lo, t_hi, first, 0, unroll=2)
        lax.fori_loop(f_lo, f_hi, second, 0, unroll=2)
        cp = pltpu.make_async_remote_copy(
            src_ref=filt_ref.at[pl.ds(f_lo, f_hi - f_lo)], dst_ref=feast.at[pl.ds(f_lo, f_hi - f_lo)],
            send_sem=fs_sem.at[c], recv_sem=fr_sem.at[c],
            device_id={"lon": west}, device_id_type=MESH)
        cp.start()
        fcopies.append((cp, f_lo, f_hi))

    def unpack(i, carry):
        f = feast[i]
        fb[2 * (nlat + i)] = f[:, 0:nb]
        fb[2 * (nlat + i) + 1] = f[:, nb:w2]
        return carry

    for cp, f_lo, f_hi in fcopies:
        cp.wait_recv()
        lax.fori_loop(f_lo, f_hi, unpack, 0, unroll=2)

    ones = jnp.ones((8, nb), BF16)
    nt = (((1,), (1,)), ((), ()))

    def foot(f, carry):
        picks = []
        for k in range(nk):
            la, lo = lat_ref[f, k], lon_ref[f, k]
            picks.append(fb[(lo // 2) * (2 * nlat) + 2 * la + lo % 2])
        y = jnp.dot(foot_w_ref[...], jnp.concatenate(picks, axis=0), preferred_element_type=F32)
        s = jnp.tanh((thr_ref[bins_ref[f]] - y) * (0.5 / tau_width))
        hi = s.astype(BF16)
        lo_part = (s - hi.astype(F32)).astype(BF16)
        row = (lax.dot_general(ones, hi, nt, preferred_element_type=F32)
               + lax.dot_general(ones, lo_part, nt, preferred_element_type=F32))
        ecdf[pl.ds(f, 1)] = 0.5 + (0.5 / nb) * row[0:1]
        return carry

    lax.fori_loop(0, nobs, foot, 0, unroll=4)

    onehot = (binscol_ref[...] == lax.broadcasted_iota(jnp.int32, (nobs, LANES), 1)).astype(F32)
    ec = ecdf[...]
    totals = jnp.sum(onehot * jnp.sum(ec, axis=1, keepdims=True), axis=0, keepdims=True)
    counts = jnp.sum(onehot, axis=0, keepdims=True) * nb
    msg[0:1] = totals
    msg[1:2] = counts
    msg[2:8] = jnp.zeros((6, LANES), F32)
    inbox[pl.ds(me, 1)] = msg[...][None]

    def tell(off, carry):
        pltpu.make_async_remote_copy(
            src_ref=msg, dst_ref=inbox.at[me], send_sem=ms_sem.at[off], recv_sem=mr_sem.at[me],
            device_id={"lon": lax.rem(me + off, n)}, device_id_type=MESH).start()
        return carry

    lax.fori_loop(1, n, tell, 0)

    def hear(off, carry):
        src = lax.rem(me + off, n)
        pltpu.make_async_remote_copy(
            src_ref=msg, dst_ref=inbox.at[src], send_sem=ms_sem.at[off], recv_sem=mr_sem.at[src],
            device_id={"lon": src}, device_id_type=MESH).wait()
        return carry

    lax.fori_loop(1, n, hear, 0)
    allsum = jnp.sum(inbox[...], axis=0)
    summary = allsum[0:1] / jnp.maximum(allsum[1:2], 1.0)
    summ_ref[...] = summary
    score_ref[...] = ec - jnp.sum(onehot * summary, axis=1, keepdims=True)

    for pair in xcopies:
        for cp in pair:
            cp.wait_send()
    for cp, _, _ in fcopies:
        cp.wait_send()


def local(n, fields, couplings, kappa, coeffs, foot_lat, foot_lon, foot_w, thresholds, bins):
    nlat, width = fields.shape[0], fields.shape[1]
    nb = couplings.shape[-1]
    nobs, nk = foot_lat.shape
    nbins = thresholds.shape[0]
    w2 = 2 * nb
    nch = 4
    x = fields.reshape(nlat, width, nb, nb).transpose(0, 2, 1, 3).reshape(nlat, nb, w2)
    kt = kappa.reshape(nlat * width, nb).T
    fw = foot_w.transpose(1, 0, 2).reshape(nb, nk * nb)
    vmem = pl.BlockSpec(memory_space=pltpu.VMEM)
    smem = pl.BlockSpec(memory_space=pltpu.SMEM)
    hbm = pl.BlockSpec(memory_space=pl.ANY)
    dma = pltpu.SemaphoreType.DMA
    filt, score, summ = pl.pallas_call(
        functools.partial(kernel, n, nlat, nb, nobs, nk, nbins, nch),
        out_shape=(
            jax.ShapeDtypeStruct((nlat, nb, w2), BF16),
            jax.ShapeDtypeStruct((nobs, nb), F32),
            jax.ShapeDtypeStruct((1, LANES), F32),
        ),
        in_specs=[vmem, vmem, hbm, vmem, vmem, smem, smem, smem, smem, smem],
        out_specs=(vmem, vmem, vmem),
        scratch_shapes=[
            pltpu.VMEM((nlat + 2, nb, w2), BF16),
            pltpu.VMEM((nlat + 2, nb, w2), BF16),
            pltpu.VMEM((nlat + 2, nb, w2), BF16),
            pltpu.VMEM((nb, nlat * width), F32),
            pltpu.VMEM((nb, nlat * width), F32),
            pltpu.VMEM(couplings.shape, BF16),
            pltpu.VMEM((nlat, 3 * nb, 3 * nb), BF16),
            pltpu.VMEM((nlat, nb, 3 * w2), F32),
            pltpu.VMEM((nlat + 2, nb, 2 * w2), BF16),
            pltpu.VMEM((nlat, nb, w2), BF16),
            pltpu.VMEM((4 * nlat, nb, nb), BF16),
            pltpu.VMEM((nobs, nb), F32),
            pltpu.VMEM((8, LANES), F32),
            pltpu.VMEM((n, 8, LANES), F32),
            dma((2, nch)), dma((2, nch)), dma((2,)), dma((2,)), dma,
            dma((nch,)), dma((nch,)), dma((n,)), dma((n,)),
        ],
        compiler_params=pltpu.CompilerParams(
            collective_id=0, has_side_effects=True, vmem_limit_bytes=40 * 1024 * 1024),
    )(x, kt, couplings, fw, bins[:, None], coeffs, foot_lat, foot_lon, thresholds, bins)
    filtered = filt.reshape(nlat, nb, width, nb).transpose(0, 2, 1, 3).reshape(nlat, width, nb * nb)
    return filtered, score, summ[0, :nbins]


def solution(mesh):
    placed = (
        P("groups", "lon", None),
        P(),
        P("groups", "lon", None),
        P(),
        P(("groups", "lon"), None),
        P(("groups", "lon"), None),
        P(),
        P(),
        P(("groups", "lon")),
    )
    return jax.shard_map(
        functools.partial(local, mesh.shape["lon"]),
        mesh=mesh,
        in_specs=placed,
        out_specs=(P("groups", "lon", None), P(("groups", "lon"), None), P("groups")),
        check_vma=False,
    )
```

time: 149 us -> 52.2 us (0.35)
  matrix products: 43.1 us -> 0 us
  Pallas kernels: 0 us -> 41.2 us
  blocking collectives: 34.1 us -> 0 us
  local copies, waits for them, and re-layouts: 34.5 us -> 10.1 us
  starting transfers between devices: 14.9 us -> 0 us
  waiting for transfers between devices: 13.2 us -> 0 us
  other arithmetic: 7.4 us -> 0 us
    dot_general x19 -> x0, matrix products: 43.1 us -> none  [the longest x18 40.6 us: apply_padded(): jnp.einsum('iab,ijbr->ijar', couplings[:, 3 * row_off + col_off], piece,...]
    pallas_call x0 -> x1, Pallas kernels: none -> 41.2 us  [local(): pl.pallas_call(functools.partial(kernel, n, nlat, nb, nobs, nk, nbins, nc...]
    psum x1 -> x0, blocking collectives: 34.1 us -> none  [local(): totals, counts = lax.psum((local_totals, local_counts), 'lon')]
    ppermute x5 -> x0, starting transfers between devices: 14.9 us -> none  [the longest x2 5.39 us: padded_2(): lax.ppermute(tail, axis, [(i, (i + 1) % count) for i in range(count)])]
    ppermute x5 -> x0, waiting for transfers between devices: 13.2 us -> none  [the longest x2 6.91 us: padded_2(): lax.ppermute(tail, axis, [(i, (i + 1) % count) for i in range(count)])]
    gather x3 -> x0, local copies, waits for them, and re-layouts: 9.03 us -> none  [footprint_terms(): picked = source[lat_index, lon_index]]
    slice x4 -> x0, local copies, waits for them, and re-layouts: 8.09 us -> none  [the longest x1 4.09 us: apply_padded(): piece = full[row_off:row_off + nlat, col_off:col_off + width]]
    concatenate x4 -> x0, other arithmetic: 6.29 us -> none  [the longest x2 5.2 us: padded_2(): jnp.concatenate([lax.ppermute(tail, axis, [(i, (i + 1) % count) for i in...]
  transfers between devices with their start and end apart: 5 -> 0, of which waited for: 2 -> 0; matrix products, arithmetic and copies ran while one was open for 3% -> 0% of each run, Pallas kernels for 0% -> 0%
where the time goes in v1:
time: 52.2 us; the launch traced here: 52.1 us
  Pallas kernels  41.2 us (79%)
  local copies, waits for them, and re-layouts  10.1 us (19%)
  between operations  0.77 us (1%)
    pallas_call x1, Pallas kernels, local(): pl.pallas_call(functools.partial(kernel, n, nlat, nb, nobs, nk, nbins, nc...  41.2 us
    reshape x3, local copies, waits for them, and re-layouts, local(): fields.reshape(nlat, width, nb, nb).transpose(0, 2, 1, 3)  3.9 us
    unnamed x19, local copies, waits for them, and re-layouts  3.14 us
    reshape x2, local copies, waits for them, and re-layouts, local(): filt.reshape(nlat, nb, width, nb).transpose(0, 2, 1, 3)  1.95 us

profile of v1, /device:TPU:0, one launch (start us, length us, event | category | flops | bytes accessed | tf_op | source)
XLA Modules:
  0.0 52.1 jit_solution(2906975603420994850)
XLA Ops:
  0.6 0.0 copy-start.4
  0.6 0.0 copy-start.5
  0.7 0.0 copy-start.1
  0.7 0.0 copy-start.6
  0.7 0.0 copy-start.7
  0.7 0.0 copy-start.2
  0.7 0.0 copy-start.3
  0.7 2.3 %reshape.24 = bf16[32,2,64,64]{3,2,1,0:T(8,128)(2,1)S(1)} reshape(bf16[32,2,4096]{2,1,0:T(2,128)(2,1)} %param.9) | data formatting | bytes 1048576 | tf_op jit(solution)/shard_map/reshape | solution.py:200
  3.1 1.1 %copy.27 = bf16[32,2,64,64]{3,1,2,0:T(2,128)(2,1)S(1)} copy(bf16[32,2,64,64]{3,2,1,0:T(8,128)(2,1)S(1)} %reshape.24) | data formatting | bytes 1048576 | tf_op jit(solution)/shard_map/reshape | solution.py:200
  4.1 0.5 reshape.25.refs_0_
  4.6 0.0 copy-done.4
  4.6 0.1 copy.21
  4.7 0.1 reshape.27.refs_3_
  4.8 0.0 copy-done.5
  4.8 0.1 copy.20
  4.9 0.0 copy-done.1
  4.9 0.1 copy.22.refs_4_
  5.0 0.0 copy-done.6
  5.0 0.1 copy.23.refs_6_
  5.1 0.0 copy-done.7
  5.1 0.1 copy.24.refs_7_
  5.2 0.0 copy-done.2
  5.2 0.0 copy-done.3
  5.2 0.0 copy-start
  5.2 2.3 %copy-done = bf16[32,9,64,64]{3,2,1,0:T(8,128)(2,1)S(1)} copy-done((bf16[32,9,64,64]{3,2,1,0:T(8,128)(2,1)S(1)}, bf16[32,9,64,64]{3,2,1,0:T(8,128)(2,1)}, u32[]{:S(2)}) %copy-start) | copy-done | bytes 2359320
  7.5 41.2 %shard_map.112 = (bf16[32,64,128]{2,1,0:T(8,128)(2,1)S(1)}, f32[32,64]{1,0:T(8,128)S(1)}, f32[1,128]{1,0:T(1,128)S(1)}) custom-call(bf16[32,64,128]{2,1,0:T(8,128)(2,1)S(1)} %reshape.25.refs_0_, f32[64,64]{1,0:T(8,128)S(1)} %bitcast.12, bf16[32,9,64,64]{3,2,1,0:T(8,128)(2,1)S(1)} %copy-done, bf16[64,256]{1,0:T(8,128)(2,1)S(1)} %reshape.27.refs_3_, ...), custom_call_target="tpu_custom_call" | custom-call | tf_op jit(solution)/shard_map/pallas_call | solution.py:207
  48.7 0.4 reshape.28
  49.1 0.3 copy.25
  49.4 1.5 %reshape.29 = bf16[32,2,4096]{2,1,0:T(2,128)(2,1)} reshape(bf16[32,2,64,64]{3,2,1,0:T(8,128)(2,1)S(1)} %copy.25) | data formatting | bytes 1048576 | tf_op jit(solution)/shard_map/reshape | solution.py:237
  50.9 0.5 slice_bitcast_fusion
  51.5 0.6 %copy.29 = f32[32,64]{1,0:T(8,128)} copy(f32[32,64]{1,0:T(8,128)S(1)} %get-tuple-element.13) | data formatting | bytes 16384
Async XLA Ops:
  0.6 4.0 %copy-start.4 = (bf16[4,64,64]{2,1,0:T(8,128)(2,1)S(1)}, bf16[4,64,64]{2,1,0:T(8,128)(2,1)}, u32[]{:S(2)}) copy-start(bf16[4,64,64]{2,1,0:T(8,128)(2,1)} %param.15) | copy-start | bytes 98308
  0.6 4.2 %copy-start.5 = (f32[32,2,64]{2,1,0:T(2,128)S(1)}, f32[32,2,64]{2,1,0:T(2,128)}, u32[]{:S(2)}) copy-start(f32[32,2,64]{2,1,0:T(2,128)} %param.11) | copy-start | bytes 49156
  0.7 4.2 %copy-start.1 = (s32[32]{0:T(128)S(1)}, s32[32]{0:T(128)}, u32[]{:S(2)}) copy-start(s32[32]{0:T(128)} %refs_9_.1) | copy-start | bytes 388
  0.7 4.3 %copy-start.6 = (s32[32,4]{0,1:T(4,128)S(1)}, s32[32,4]{0,1:T(4,128)}, u32[]{:S(2)}) copy-start(s32[32,4]{0,1:T(4,128)} %param.13) | copy-start | bytes 1540
  0.7 4.4 %copy-start.7 = (s32[32,4]{0,1:T(4,128)S(1)}, s32[32,4]{0,1:T(4,128)}, u32[]{:S(2)}) copy-start(s32[32,4]{0,1:T(4,128)} %param.14) | copy-start | bytes 1540
  0.7 4.5 %copy-start.2 = (f32[3]{0:T(128)S(1)}, f32[3]{0:T(128)}, u32[]{:S(2)}) copy-start(f32[3]{0:T(128)} %refs_5_.1) | copy-start | bytes 40
  0.7 4.5 %copy-start.3 = (f32[16]{0:T(128)S(1)}, f32[16]{0:T(128)}, u32[]{:S(2)}) copy-start(f32[16]{0:T(128)} %refs_8_.1) | copy-start | bytes 196
  5.2 2.3 %copy-start = (bf16[32,9,64,64]{3,2,1,0:T(8,128)(2,1)S(1)}, bf16[32,9,64,64]{3,2,1,0:T(8,128)(2,1)}, u32[]{:S(2)}) copy-start(bf16[32,9,64,64]{3,2,1,0:T(8,128)(2,1)} %refs_2_.1) | copy-start | bytes 7077892

commit v2 on v1

--- a/solution.py
+++ b/solution.py
@@ -17,7 +17,7 @@
 def kernel(n, nlat, nb, nobs, nk, nbins, nch, *refs):
     (x_ref, kt_ref, coup_hbm, foot_w_ref, binscol_ref, coef_ref, lat_ref, lon_ref, thr_ref, bins_ref,
      filt_ref, score_ref, summ_ref,
-     xw, xo, xe, kw, ke, coup, wc, kx, t1, feast, fb, ecdf, msg, inbox,
+     xw, xe, xc, kw, ke, coup, wc, kx, t1, fown, feast, fb, ecdf, msg, inbox,
      xs_sem, xr_sem, ks_sem, kr_sem, c_sem, fs_sem, fr_sem, ms_sem, mr_sem) = refs
     me = lax.axis_index("lon")
     east, west = lax.rem(me + 1, n), lax.rem(me + n - 1, n)
@@ -47,20 +47,38 @@
         pair = []
         for side, (dst, dev) in enumerate(((xw, east), (xe, west))):
             cp = pltpu.make_async_remote_copy(
-                src_ref=x_ref.at[pl.ds(c * ch, ch)], dst_ref=dst.at[pl.ds(1 + c * ch, ch)],
+                src_ref=x_ref.at[pl.ds(c * ch, ch)], dst_ref=dst.at[pl.ds(c * ch, ch)],
                 send_sem=xs_sem.at[side, c], recv_sem=xr_sem.at[side, c],
                 device_id={"lon": dev}, device_id_type=MESH)
             cp.start()
             pair.append(cp)
         xcopies.append(pair)
 
-    zero = jnp.zeros((nb, w2), BF16)
-    for buf in (xw, xo, xe):
-        buf[0] = zero
-        buf[nlat + 1] = zero
+    xc[0] = jnp.zeros((nb, 3 * w2), BF16)
+    xc[nlat + 1] = jnp.zeros((nb, 3 * w2), BF16)
     t1[0] = jnp.zeros((nb, 2 * w2), BF16)
     t1[nlat + 1] = jnp.zeros((nb, 2 * w2), BF16)
-    xo[pl.ds(1, nlat)] = x_ref[...]
+
+    rows = lax.broadcasted_iota(jnp.int32, (nb, nb), 0)
+    cols = lax.broadcasted_iota(jnp.int32, (nb, nb), 1)
+    swap = (rows + 1 - 2 * (rows % 2) == cols).astype(F32).astype(BF16)
+    lane_hi = (lax.broadcasted_iota(jnp.int32, (nb, w2), 1) >= nb).astype(jnp.int32)
+    keep = lax.broadcasted_iota(jnp.int32, (nb, w2), 0) % 2 == lane_hi
+
+    def turned(v):
+        other = jnp.dot(swap, v, preferred_element_type=F32)
+        return jnp.where(keep, v.astype(F32), pltpu.roll(other, nb, 1)).astype(BF16)
+
+    def turn_own(i, carry):
+        xc[i + 1, :, w2:2 * w2] = turned(x_ref[i])
+        return carry
+
+    lax.fori_loop(0, nlat, turn_own, 0, unroll=4)
+
+    def turn_sides(i, carry):
+        xc[i + 1, :, 0:w2] = turned(xw[i])
+        xc[i + 1, :, 2 * w2:3 * w2] = turned(xe[i])
+        return carry
 
     c_copy.wait()
 
@@ -87,10 +105,8 @@
     c0, c1, c2 = coef_ref[0], coef_ref[1], coef_ref[2]
 
     def first(i, carry):
-        rhs = jnp.concatenate(
-            [buf[pl.ds(i, 3)].reshape(3 * nb, w2) for buf in (xw, xo, xe)], axis=1)
-        p = jnp.dot(wc[i], rhs, preferred_element_type=F32)
-        centre = jnp.concatenate([buf[i + 1].astype(F32) for buf in (xw, xo, xe)], axis=1)
+        p = jnp.dot(wc[i], xc[pl.ds(i, 3)].reshape(3 * nb, 3 * w2), preferred_element_type=F32)
+        centre = xc[i + 1].astype(F32)
         mid = p[nb:2 * nb] + kx[i] * centre
         total = p[0:nb, 0:2 * w2] + p[2 * nb:3 * nb, w2:3 * w2] + mid[:, nb:nb + 2 * w2]
         t1[i + 1] = total.astype(BF16)
@@ -101,9 +117,9 @@
         own = t1[i + 1].astype(F32)[:, nb:nb + w2]
         st = (p[0:nb, 0:w2] + p[2 * nb:3 * nb, w2:2 * w2] + p[nb:2 * nb, nb:nb + w2]
               + kx[i, :, w2:2 * w2] * own)
-        x = x_ref[i].astype(F32)
+        x = xc[i + 1, :, w2:2 * w2].astype(F32)
         f = (c0 * x + c1 * own + c2 * (2.0 * st - x)).astype(BF16)
-        filt_ref[i] = f
+        fown[i] = f
         fb[2 * i] = f[:, 0:nb]
         fb[2 * i + 1] = f[:, nb:w2]
         return carry
@@ -115,14 +131,21 @@
         last = c == nch - 1
         t_lo, t_hi = max(c * ch - 1, 0), nlat if last else (c + 1) * ch - 1
         f_lo, f_hi = max(c * ch - 2, 0), nlat if last else (c + 1) * ch - 2
+        lax.fori_loop(c * ch, (c + 1) * ch, turn_sides, 0, unroll=2)
         lax.fori_loop(t_lo, t_hi, first, 0, unroll=2)
         lax.fori_loop(f_lo, f_hi, second, 0, unroll=2)
         cp = pltpu.make_async_remote_copy(
-            src_ref=filt_ref.at[pl.ds(f_lo, f_hi - f_lo)], dst_ref=feast.at[pl.ds(f_lo, f_hi - f_lo)],
+            src_ref=fown.at[pl.ds(f_lo, f_hi - f_lo)], dst_ref=feast.at[pl.ds(f_lo, f_hi - f_lo)],
             send_sem=fs_sem.at[c], recv_sem=fr_sem.at[c],
             device_id={"lon": west}, device_id_type=MESH)
         cp.start()
         fcopies.append((cp, f_lo, f_hi))
+
+    def turn_out(i, carry):
+        filt_ref[i] = turned(fown[i])
+        return carry
+
+    lax.fori_loop(0, nlat, turn_out, 0, unroll=4)
 
     def unpack(i, carry):
         f = feast[i]
@@ -197,12 +220,13 @@
     nbins = thresholds.shape[0]
     w2 = 2 * nb
     nch = 4
-    x = fields.reshape(nlat, width, nb, nb).transpose(0, 2, 1, 3).reshape(nlat, nb, w2)
+    halves = nb * nb // w2
+    x = fields.reshape(nlat, width, halves, w2).transpose(0, 2, 1, 3).reshape(nlat, nb, w2)
     kt = kappa.reshape(nlat * width, nb).T
     fw = foot_w.transpose(1, 0, 2).reshape(nb, nk * nb)
     vmem = pl.BlockSpec(memory_space=pltpu.VMEM)
     smem = pl.BlockSpec(memory_space=pltpu.SMEM)
-    hbm = pl.BlockSpec(memory_space=pl.ANY)
+    hbm = pl.BlockSpec(memory_space=pltpu.HBM)
     dma = pltpu.SemaphoreType.DMA
     filt, score, summ = pl.pallas_call(
         functools.partial(kernel, n, nlat, nb, nobs, nk, nbins, nch),
@@ -214,15 +238,16 @@
         in_specs=[vmem, vmem, hbm, vmem, vmem, smem, smem, smem, smem, smem],
         out_specs=(vmem, vmem, vmem),
         scratch_shapes=[
-            pltpu.VMEM((nlat + 2, nb, w2), BF16),
-            pltpu.VMEM((nlat + 2, nb, w2), BF16),
-            pltpu.VMEM((nlat + 2, nb, w2), BF16),
+            pltpu.VMEM((nlat, nb, w2), BF16),
+            pltpu.VMEM((nlat, nb, w2), BF16),
+            pltpu.VMEM((nlat + 2, nb, 3 * w2), BF16),
             pltpu.VMEM((nb, nlat * width), F32),
             pltpu.VMEM((nb, nlat * width), F32),
             pltpu.VMEM(couplings.shape, BF16),
             pltpu.VMEM((nlat, 3 * nb, 3 * nb), BF16),
             pltpu.VMEM((nlat, nb, 3 * w2), F32),
             pltpu.VMEM((nlat + 2, nb, 2 * w2), BF16),
+            pltpu.VMEM((nlat, nb, w2), BF16),
             pltpu.VMEM((nlat, nb, w2), BF16),
             pltpu.VMEM((4 * nlat, nb, nb), BF16),
             pltpu.VMEM((nobs, nb), F32),
@@ -232,9 +257,9 @@
             dma((nch,)), dma((nch,)), dma((n,)), dma((n,)),
         ],
         compiler_params=pltpu.CompilerParams(
-            collective_id=0, has_side_effects=True, vmem_limit_bytes=40 * 1024 * 1024),
+            collective_id=0, has_side_effects=True, vmem_limit_bytes=60 * 1024 * 1024),
     )(x, kt, couplings, fw, bins[:, None], coeffs, foot_lat, foot_lon, thresholds, bins)
-    filtered = filt.reshape(nlat, nb, width, nb).transpose(0, 2, 1, 3).reshape(nlat, width, nb * nb)
+    filtered = filt.reshape(nlat, halves, width, w2).transpose(0, 2, 1, 3).reshape(nlat, width, nb * nb)
     return filtered, score, summ[0, :nbins]
 
 

time: 52.2 us -> 56.7 us (1.086)
  Pallas kernels: 41.2 us -> 43.7 us
  local copies, waits for them, and re-layouts: 10.1 us -> 11.9 us
    reshape x5 -> x0, local copies, waits for them, and re-layouts: 5.85 us -> none  [the longest x3 3.9 us: local(): fields.reshape(nlat, width, nb, nb).transpose(0, 2, 1, 3)]
    unnamed x19 -> x4, local copies, waits for them, and re-layouts: 3.14 us -> 6.32 us
    pallas_call x1, Pallas kernels: 41.2 us -> 43.7 us  [local(): pl.pallas_call(functools.partial(kernel, n, nlat, nb, nobs, nk, nbins, nc...]
    reshape x1, local copies, waits for them, and re-layouts: 0.07 us -> 1.45 us  [local(): kt = kappa.reshape(nlat * width, nb).T]
    broadcast_in_dim x1, local copies, waits for them, and re-layouts: 0.09 us -> 1.34 us  [local(): bins[:, None]]
    transpose x1, local copies, waits for them, and re-layouts: 0.05 us -> 0.89 us  [local(): fw = foot_w.transpose(1, 0, 2).reshape(nb, nk * nb)]
    squeeze x1, local copies, waits for them, and re-layouts: 0.51 us -> 1.17 us  [local(): return (filtered, score, summ[0, :nbins])]
    reshape x1, local copies, waits for them, and re-layouts: 0.11 us -> 0.73 us  [local(): fw = foot_w.transpose(1, 0, 2).reshape(nb, nk * nb)]
where the time goes in v2:
time: 56.7 us; the launch traced here: 56.2 us
  Pallas kernels  43.7 us (77%)
  local copies, waits for them, and re-layouts  11.9 us (21%)
  between operations  0.64 us (1%)
    pallas_call x1, Pallas kernels, local(): pl.pallas_call(functools.partial(kernel, n, nlat, nb, nobs, nk, nbins, nc...  43.7 us
    unnamed x4, local copies, waits for them, and re-layouts  6.32 us
    reshape x1, local copies, waits for them, and re-layouts, local(): kt = kappa.reshape(nlat * width, nb).T  1.45 us
    broadcast_in_dim x1, local copies, waits for them, and re-layouts, local(): bins[:, None]  1.34 us
    squeeze x1, local copies, waits for them, and re-layouts, local(): return (filtered, score, summ[0, :nbins])  1.17 us

profile of v2, /device:TPU:0, one launch (start us, length us, event | category | flops | bytes accessed | tf_op | source)
XLA Modules:
  0.0 56.2 jit_solution(12536483883661057094)
XLA Ops:
  0.6 1.4 %copy.23.refs_6_ = s32[32,4]{1,0:T(8,128)} copy(s32[32,4]{0,1:T(4,128)} %param.13) | data formatting | bytes 1024 | tf_op args[4]
  2.0 1.4 %copy.24.refs_7_ = s32[32,4]{1,0:T(8,128)} copy(s32[32,4]{0,1:T(4,128)} %param.14) | data formatting | bytes 1024 | tf_op args[5]
  3.3 1.3 %copy.22.refs_4_ = s32[32,1]{1,0:T(8,128)} copy(s32[32,1]{0,1:T(1,128)} %bitcast.21) | data formatting | bytes 256 | tf_op jit(solution)/shard_map/broadcast_in_dim | solution.py:261
  4.7 1.5 %copy.20 = f32[64,64]{0,1:T(8,128)} copy(f32[64,64]{1,0:T(8,128)} %bitcast.20) | data formatting | bytes 32768 | tf_op jit(solution)/shard_map/reshape | solution.py:225
  6.1 0.9 %copy.21 = bf16[64,4,64]{2,1,0:T(4,128)(2,1)S(1)} copy(bf16[64,4,64]{2,0,1:T(8,128)(2,1)} %bitcast.19) | data formatting | bytes 65536 | tf_op jit(solution)/shard_map/transpose | solution.py:226
  7.0 0.7 %reshape.27.refs_3_ = bf16[64,256]{1,0:T(8,128)(2,1)} reshape(bf16[64,4,64]{2,1,0:T(4,128)(2,1)S(1)} %copy.21) | data formatting | bytes 65536 | tf_op jit(solution)/shard_map/reshape | solution.py:226
  7.8 43.7 %shard_map.112 = (bf16[32,64,128]{2,1,0:T(8,128)(2,1)}, f32[32,64]{1,0:T(8,128)}, f32[1,128]{1,0:T(1,128)}) custom-call(bf16[32,64,128]{2,1,0:T(8,128)(2,1)} %bitcast.16, f32[64,64]{1,0:T(8,128)} %bitcast.18, bf16[32,9,64,64]{3,2,1,0:T(8,128)(2,1)} %refs_2_.1, bf16[64,256]{1,0:T(8,128)(2,1)} %reshape.27.refs_3_, s32[32,1]{1,0:T(8,128)} %copy.22.refs_4_, ...), custom_call_target="tpu_custom_call" | custom-call | tf_op jit(solution)/shard_map/pallas_call | solution.py:231
  51.5 1.2 %slice_bitcast_fusion = f32[16]{0:T(128)} fusion(f32[1,128]{1,0:T(1,128)} %get-tuple-element.8), kind=kLoop, calls=%fused_computation | loop fusion | bytes 128 | tf_op jit(solution)/shard_map/squeeze | solution.py:263
  52.6 2.3 %copy.28 = bf16[32,2,4096]{2,1,0:T(2,128)(2,1)} copy(bf16[32,2,4096]{2,1,0:T(2,128)(2,1)} %bitcast.17) | data formatting | bytes 1048576
  54.9 1.3 %copy.29 = f32[32,64]{1,0:T(8,128)} copy(f32[32,64]{1,0:T(8,128)} %get-tuple-element.13) | data formatting | bytes 16384

commit v3 on v2

--- a/solution.py
+++ b/solution.py
@@ -15,9 +15,9 @@
 
 
 def kernel(n, nlat, nb, nobs, nk, nbins, nch, *refs):
-    (x_ref, kt_ref, coup_hbm, foot_w_ref, binscol_ref, coef_ref, lat_ref, lon_ref, thr_ref, bins_ref,
+    (x_ref, kt_ref, coup_hbm, foot_w_ref, coef_ref, lat_ref, lon_ref, thr_ref, bins_ref,
      filt_ref, score_ref, summ_ref,
-     xw, xe, xc, kw, ke, coup, wc, kx, t1, fown, feast, fb, ecdf, msg, inbox,
+     xw, xe, xc, kw, ke, coup, wc, kx, t1, fown, feast, fb, fw, hot, ecdf, msg, inbox,
      xs_sem, xr_sem, ks_sem, kr_sem, c_sem, fs_sem, fr_sem, ms_sem, mr_sem) = refs
     me = lax.axis_index("lon")
     east, west = lax.rem(me + 1, n), lax.rem(me + n - 1, n)
@@ -91,7 +91,7 @@
 
     for cp in kcopies:
         cp.wait()
-    kwv, kov, kev = kw[...], kt_ref[...], ke[...]
+    kwv, kov, kev = (jnp.transpose(v[...]) for v in (kw, kt_ref, ke))
     low = lax.broadcasted_iota(jnp.int32, (nb, w2), 1) < nb
 
     def spread(v, j):
@@ -101,6 +101,12 @@
         kx[i, :, 0:w2] = spread(kwv, 2 * i + 1)
         kx[i, :, w2:2 * w2] = jnp.where(low, spread(kov, 2 * i), spread(kov, 2 * i + 1))
         kx[i, :, 2 * w2:3 * w2] = spread(kev, 2 * i)
+
+    fw[...] = jnp.concatenate([foot_w_ref[k] for k in range(nk)], axis=1)
+    ones = jnp.ones((8, nb), BF16)
+    bin_ids = lax.broadcasted_iota(jnp.int32, (1, LANES), 1)
+    for f in range(nobs):
+        hot[f:f + 1] = (bin_ids == bins_ref[f]).astype(F32)
 
     c0, c1, c2 = coef_ref[0], coef_ref[1], coef_ref[2]
 
@@ -157,15 +163,14 @@
         cp.wait_recv()
         lax.fori_loop(f_lo, f_hi, unpack, 0, unroll=2)
 
-    ones = jnp.ones((8, nb), BF16)
     nt = (((1,), (1,)), ((), ()))
 
     def foot(f, carry):
         picks = []
         for k in range(nk):
-            la, lo = lat_ref[f, k], lon_ref[f, k]
+            la, lo = lat_ref[k, f], lon_ref[k, f]
             picks.append(fb[(lo // 2) * (2 * nlat) + 2 * la + lo % 2])
-        y = jnp.dot(foot_w_ref[...], jnp.concatenate(picks, axis=0), preferred_element_type=F32)
+        y = jnp.dot(fw[...], jnp.concatenate(picks, axis=0), preferred_element_type=F32)
         s = jnp.tanh((thr_ref[bins_ref[f]] - y) * (0.5 / tau_width))
         hi = s.astype(BF16)
         lo_part = (s - hi.astype(F32)).astype(BF16)
@@ -176,7 +181,7 @@
 
     lax.fori_loop(0, nobs, foot, 0, unroll=4)
 
-    onehot = (binscol_ref[...] == lax.broadcasted_iota(jnp.int32, (nobs, LANES), 1)).astype(F32)
+    onehot = hot[...]
     ec = ecdf[...]
     totals = jnp.sum(onehot * jnp.sum(ec, axis=1, keepdims=True), axis=0, keepdims=True)
     counts = jnp.sum(onehot, axis=0, keepdims=True) * nb
@@ -222,8 +227,7 @@
     nch = 4
     halves = nb * nb // w2
     x = fields.reshape(nlat, width, halves, w2).transpose(0, 2, 1, 3).reshape(nlat, nb, w2)
-    kt = kappa.reshape(nlat * width, nb).T
-    fw = foot_w.transpose(1, 0, 2).reshape(nb, nk * nb)
+    kt = kappa.reshape(nlat * width, nb)
     vmem = pl.BlockSpec(memory_space=pltpu.VMEM)
     smem = pl.BlockSpec(memory_space=pltpu.SMEM)
     hbm = pl.BlockSpec(memory_space=pltpu.HBM)
@@ -235,14 +239,14 @@
             jax.ShapeDtypeStruct((nobs, nb), F32),
             jax.ShapeDtypeStruct((1, LANES), F32),
         ),
-        in_specs=[vmem, vmem, hbm, vmem, vmem, smem, smem, smem, smem, smem],
+        in_specs=[vmem, vmem, hbm, vmem, smem, smem, smem, smem, smem],
         out_specs=(vmem, vmem, vmem),
         scratch_shapes=[
             pltpu.VMEM((nlat, nb, w2), BF16),
             pltpu.VMEM((nlat, nb, w2), BF16),
             pltpu.VMEM((nlat + 2, nb, 3 * w2), BF16),
-            pltpu.VMEM((nb, nlat * width), F32),
-            pltpu.VMEM((nb, nlat * width), F32),
+            pltpu.VMEM((nlat * width, nb), F32),
+            pltpu.VMEM((nlat * width, nb), F32),
             pltpu.VMEM(couplings.shape, BF16),
             pltpu.VMEM((nlat, 3 * nb, 3 * nb), BF16),
             pltpu.VMEM((nlat, nb, 3 * w2), F32),
@@ -250,6 +254,8 @@
             pltpu.VMEM((nlat, nb, w2), BF16),
             pltpu.VMEM((nlat, nb, w2), BF16),
             pltpu.VMEM((4 * nlat, nb, nb), BF16),
+            pltpu.VMEM((nb, nk * nb), BF16),
+            pltpu.VMEM((nobs, LANES), F32),
             pltpu.VMEM((nobs, nb), F32),
             pltpu.VMEM((8, LANES), F32),
             pltpu.VMEM((n, 8, LANES), F32),
@@ -257,8 +263,8 @@
             dma((nch,)), dma((nch,)), dma((n,)), dma((n,)),
         ],
         compiler_params=pltpu.CompilerParams(
-            collective_id=0, has_side_effects=True, vmem_limit_bytes=60 * 1024 * 1024),
-    )(x, kt, couplings, fw, bins[:, None], coeffs, foot_lat, foot_lon, thresholds, bins)
+            collective_id=0, has_side_effects=True, vmem_limit_bytes=50 * 1024 * 1024),
+    )(x, kt, couplings, foot_w, coeffs, foot_lat.T, foot_lon.T, thresholds, bins)
     filtered = filt.reshape(nlat, halves, width, w2).transpose(0, 2, 1, 3).reshape(nlat, width, nb * nb)
     return filtered, score, summ[0, :nbins]
 

time: 56.7 us -> 51 us (0.90)
  local copies, waits for them, and re-layouts: 11.9 us -> 7.87 us
  Pallas kernels: 43.7 us -> 42.1 us
    reshape x2 -> x0, local copies, waits for them, and re-layouts: 2.18 us -> none  [the longest x1 1.45 us: local(): kt = kappa.reshape(nlat * width, nb).T]
    pallas_call x1, Pallas kernels: 43.7 us -> 42.1 us  [local(): pl.pallas_call(functools.partial(kernel, n, nlat, nb, nobs, nk, nbins, nc...]
    broadcast_in_dim x1 -> x0, local copies, waits for them, and re-layouts: 1.34 us -> none  [local(): bins[:, None]]
    unnamed x4 -> x18, local copies, waits for them, and re-layouts: 6.32 us -> 7.35 us
    transpose x1 -> x0, local copies, waits for them, and re-layouts: 0.89 us -> none  [local(): fw = foot_w.transpose(1, 0, 2).reshape(nb, nk * nb)]
    squeeze x1, local copies, waits for them, and re-layouts: 1.17 us -> 0.51 us  [local(): return (filtered, score, summ[0, :nbins])]
where the time goes in v3:
time: 51 us; the launch traced here: 50.6 us
  Pallas kernels  42.1 us (83%)
  local copies, waits for them, and re-layouts  7.87 us (15%)
  between operations  0.66 us (1%)
    pallas_call x1, Pallas kernels, local(): pl.pallas_call(functools.partial(kernel, n, nlat, nb, nobs, nk, nbins, nc...  42.1 us
    unnamed x18, local copies, waits for them, and re-layouts  7.35 us

profile of v3, /device:TPU:0, one launch (start us, length us, event | category | flops | bytes accessed | tf_op | source)
XLA Modules:
  0.0 50.6 jit_solution(4412651095416102416)
XLA Ops:
  0.6 0.0 copy-start
  0.6 1.0 %copy-done = bf16[32,2,4096]{2,1,0:T(2,128)(2,1)S(1)} copy-done((bf16[32,2,4096]{2,1,0:T(2,128)(2,1)S(1)}, bf16[32,2,4096]{2,1,0:T(2,128)(2,1)}, u32[]{:S(2)}) %copy-start) | copy-done | bytes 524312
  1.7 0.0 copy-start.1
  1.7 0.8 %copy-done.1 = bf16[4,64,64]{2,1,0:T(8,128)(2,1)S(1)} copy-done((bf16[4,64,64]{2,1,0:T(8,128)(2,1)S(1)}, bf16[4,64,64]{2,1,0:T(8,128)(2,1)}, u32[]{:S(2)}) %copy-start.1) | copy-done | bytes 32792
  2.5 0.0 copy-start.2
  2.5 0.8 %copy-done.2 = f32[32,2,64]{2,1,0:T(2,128)S(1)} copy-done((f32[32,2,64]{2,1,0:T(2,128)S(1)}, f32[32,2,64]{2,1,0:T(2,128)}, u32[]{:S(2)}) %copy-start.2) | copy-done | bytes 16408
  3.3 0.0 copy-start.3
  3.3 0.7 %copy-done.3 = s32[32,4]{0,1:T(4,128)S(1)} copy-done((s32[32,4]{0,1:T(4,128)S(1)}, s32[32,4]{0,1:T(4,128)}, u32[]{:S(2)}) %copy-start.3) | copy-done | bytes 536
  4.0 0.0 copy-start.4
  4.0 0.7 %copy-done.4 = s32[32,4]{0,1:T(4,128)S(1)} copy-done((s32[32,4]{0,1:T(4,128)S(1)}, s32[32,4]{0,1:T(4,128)}, u32[]{:S(2)}) %copy-start.4) | copy-done | bytes 536
  4.6 0.0 copy-start.5
  4.6 0.7 %copy-done.5 = f32[3]{0:T(128)S(1)} copy-done((f32[3]{0:T(128)S(1)}, f32[3]{0:T(128)}, u32[]{:S(2)}) %copy-start.5) | copy-done | bytes 36
  5.3 0.0 copy-start.6
  5.3 0.7 %copy-done.6 = f32[16]{0:T(128)S(1)} copy-done((f32[16]{0:T(128)S(1)}, f32[16]{0:T(128)}, u32[]{:S(2)}) %copy-start.6) | copy-done | bytes 88
  6.0 0.0 copy-start.7
  6.0 0.7 %copy-done.7 = s32[32]{0:T(128)S(1)} copy-done((s32[32]{0:T(128)S(1)}, s32[32]{0:T(128)}, u32[]{:S(2)}) %copy-start.7) | copy-done | bytes 152
  6.6 42.1 %shard_map.112 = (bf16[32,64,128]{2,1,0:T(8,128)(2,1)S(1)}, f32[32,64]{1,0:T(8,128)S(1)}, f32[1,128]{1,0:T(1,128)S(1)}) custom-call(bf16[32,64,128]{2,1,0:T(8,128)(2,1)S(1)} %bitcast.16, f32[64,64]{1,0:T(8,128)S(1)} %bitcast.17, bf16[32,9,64,64]{3,2,1,0:T(8,128)(2,1)} %refs_2_.1, bf16[4,64,64]{2,1,0:T(8,128)(2,1)S(1)} %copy-done.1, f32[3]{0:T(128)S(1)} %copy-done.5, ...), custom_call_target="tpu_custom_call" | custom-call | tf_op jit(solution)/shard_map/pallas_call | solution.py:235
  48.7 0.5 %slice_bitcast_fusion = f32[16]{0:T(128)} fusion(f32[1,128]{1,0:T(1,128)S(1)} %get-tuple-element.8), kind=kLoop, calls=%fused_computation | loop fusion | bytes 128 | tf_op jit(solution)/shard_map/squeeze | solution.py:269
  49.2 0.8 %copy.16 = bf16[32,2,4096]{2,1,0:T(2,128)(2,1)} copy(bf16[32,2,4096]{2,1,0:T(2,128)(2,1)S(1)} %bitcast.15) | data formatting | bytes 1048576
  50.0 0.6 %copy.17 = f32[32,64]{1,0:T(8,128)} copy(f32[32,64]{1,0:T(8,128)S(1)} %get-tuple-element.13) | data formatting | bytes 16384
Async XLA Ops:
  0.6 1.0 %copy-start = (bf16[32,2,4096]{2,1,0:T(2,128)(2,1)S(1)}, bf16[32,2,4096]{2,1,0:T(2,128)(2,1)}, u32[]{:S(2)}) copy-start(bf16[32,2,4096]{2,1,0:T(2,128)(2,1)} %param.9) | copy-start | bytes 1572868
  1.7 0.8 %copy-start.1 = (bf16[4,64,64]{2,1,0:T(8,128)(2,1)S(1)}, bf16[4,64,64]{2,1,0:T(8,128)(2,1)}, u32[]{:S(2)}) copy-start(bf16[4,64,64]{2,1,0:T(8,128)(2,1)} %refs_3_.1) | copy-start | bytes 98308
  2.5 0.8 %copy-start.2 = (f32[32,2,64]{2,1,0:T(2,128)S(1)}, f32[32,2,64]{2,1,0:T(2,128)}, u32[]{:S(2)}) copy-start(f32[32,2,64]{2,1,0:T(2,128)} %param.11) | copy-start | bytes 49156
  3.3 0.7 %copy-start.3 = (s32[32,4]{0,1:T(4,128)S(1)}, s32[32,4]{0,1:T(4,128)}, u32[]{:S(2)}) copy-start(s32[32,4]{0,1:T(4,128)} %param.13) | copy-start | bytes 1540
  4.0 0.7 %copy-start.4 = (s32[32,4]{0,1:T(4,128)S(1)}, s32[32,4]{0,1:T(4,128)}, u32[]{:S(2)}) copy-start(s32[32,4]{0,1:T(4,128)} %param.14) | copy-start | bytes 1540
  4.6 0.7 %copy-start.5 = (f32[3]{0:T(128)S(1)}, f32[3]{0:T(128)}, u32[]{:S(2)}) copy-start(f32[3]{0:T(128)} %refs_4_.1) | copy-start | bytes 40
  5.3 0.7 %copy-start.6 = (f32[16]{0:T(128)S(1)}, f32[16]{0:T(128)}, u32[]{:S(2)}) copy-start(f32[16]{0:T(128)} %refs_7_.1) | copy-start | bytes 196
  6.0 0.7 %copy-start.7 = (s32[32]{0:T(128)S(1)}, s32[32]{0:T(128)}, u32[]{:S(2)}) copy-start(s32[32]{0:T(128)} %refs_8_.1) | copy-start | bytes 388

commit v4 on v3

--- a/solution.py
+++ b/solution.py
@@ -137,9 +137,9 @@
         last = c == nch - 1
         t_lo, t_hi = max(c * ch - 1, 0), nlat if last else (c + 1) * ch - 1
         f_lo, f_hi = max(c * ch - 2, 0), nlat if last else (c + 1) * ch - 2
-        lax.fori_loop(c * ch, (c + 1) * ch, turn_sides, 0, unroll=2)
-        lax.fori_loop(t_lo, t_hi, first, 0, unroll=2)
-        lax.fori_loop(f_lo, f_hi, second, 0, unroll=2)
+        lax.fori_loop(c * ch, (c + 1) * ch, turn_sides, 0, unroll=4)
+        lax.fori_loop(t_lo, t_hi, first, 0, unroll=4)
+        lax.fori_loop(f_lo, f_hi, second, 0, unroll=4)
         cp = pltpu.make_async_remote_copy(
             src_ref=fown.at[pl.ds(f_lo, f_hi - f_lo)], dst_ref=feast.at[pl.ds(f_lo, f_hi - f_lo)],
             send_sem=fs_sem.at[c], recv_sem=fr_sem.at[c],
@@ -179,7 +179,7 @@
         ecdf[pl.ds(f, 1)] = 0.5 + (0.5 / nb) * row[0:1]
         return carry
 
-    lax.fori_loop(0, nobs, foot, 0, unroll=4)
+    lax.fori_loop(0, nobs, foot, 0, unroll=8)
 
     onehot = hot[...]
     ec = ecdf[...]
@@ -224,7 +224,7 @@
     nobs, nk = foot_lat.shape
     nbins = thresholds.shape[0]
     w2 = 2 * nb
-    nch = 4
+    nch = 8
     halves = nb * nb // w2
     x = fields.reshape(nlat, width, halves, w2).transpose(0, 2, 1, 3).reshape(nlat, nb, w2)
     kt = kappa.reshape(nlat * width, nb)

time: 51 us -> 47.6 us (0.933)
  Pallas kernels: 42.1 us -> 38.8 us
    pallas_call x1, Pallas kernels: 42.1 us -> 38.8 us  [local(): pl.pallas_call(functools.partial(kernel, n, nlat, nb, nobs, nk, nbins, nc...]
where the time goes in v4:
time: 47.6 us; the launch traced here: 47.3 us
  Pallas kernels  38.8 us (82%)
  local copies, waits for them, and re-layouts  7.87 us (17%)
  between operations  0.66 us (1%)
    pallas_call x1, Pallas kernels, local(): pl.pallas_call(functools.partial(kernel, n, nlat, nb, nobs, nk, nbins, nc...  38.8 us
    unnamed x18, local copies, waits for them, and re-layouts  7.35 us

profile of v4, /device:TPU:0, one launch (start us, length us, event | category | flops | bytes accessed | tf_op | source)
XLA Modules:
  0.0 47.3 jit_solution(8311659873789127349)
XLA Ops:
  0.6 0.0 copy-start
  0.6 1.0 %copy-done = bf16[32,2,4096]{2,1,0:T(2,128)(2,1)S(1)} copy-done((bf16[32,2,4096]{2,1,0:T(2,128)(2,1)S(1)}, bf16[32,2,4096]{2,1,0:T(2,128)(2,1)}, u32[]{:S(2)}) %copy-start) | copy-done | bytes 524312
  1.7 0.0 copy-start.1
  1.7 0.8 %copy-done.1 = bf16[4,64,64]{2,1,0:T(8,128)(2,1)S(1)} copy-done((bf16[4,64,64]{2,1,0:T(8,128)(2,1)S(1)}, bf16[4,64,64]{2,1,0:T(8,128)(2,1)}, u32[]{:S(2)}) %copy-start.1) | copy-done | bytes 32792
  2.5 0.0 copy-start.2
  2.5 0.8 %copy-done.2 = f32[32,2,64]{2,1,0:T(2,128)S(1)} copy-done((f32[32,2,64]{2,1,0:T(2,128)S(1)}, f32[32,2,64]{2,1,0:T(2,128)}, u32[]{:S(2)}) %copy-start.2) | copy-done | bytes 16408
  3.3 0.0 copy-start.3
  3.3 0.7 %copy-done.3 = s32[32,4]{0,1:T(4,128)S(1)} copy-done((s32[32,4]{0,1:T(4,128)S(1)}, s32[32,4]{0,1:T(4,128)}, u32[]{:S(2)}) %copy-start.3) | copy-done | bytes 536
  4.0 0.0 copy-start.4
  4.0 0.7 %copy-done.4 = s32[32,4]{0,1:T(4,128)S(1)} copy-done((s32[32,4]{0,1:T(4,128)S(1)}, s32[32,4]{0,1:T(4,128)}, u32[]{:S(2)}) %copy-start.4) | copy-done | bytes 536
  4.6 0.0 copy-start.5
  4.6 0.7 %copy-done.5 = f32[3]{0:T(128)S(1)} copy-done((f32[3]{0:T(128)S(1)}, f32[3]{0:T(128)}, u32[]{:S(2)}) %copy-start.5) | copy-done | bytes 36
  5.3 0.0 copy-start.6
  5.3 0.7 %copy-done.6 = f32[16]{0:T(128)S(1)} copy-done((f32[16]{0:T(128)S(1)}, f32[16]{0:T(128)}, u32[]{:S(2)}) %copy-start.6) | copy-done | bytes 88
  6.0 0.0 copy-start.7
  6.0 0.7 %copy-done.7 = s32[32]{0:T(128)S(1)} copy-done((s32[32]{0:T(128)S(1)}, s32[32]{0:T(128)}, u32[]{:S(2)}) %copy-start.7) | copy-done | bytes 152
  6.6 38.8 %shard_map.112 = (bf16[32,64,128]{2,1,0:T(8,128)(2,1)S(1)}, f32[32,64]{1,0:T(8,128)S(1)}, f32[1,128]{1,0:T(1,128)S(1)}) custom-call(bf16[32,64,128]{2,1,0:T(8,128)(2,1)S(1)} %bitcast.16, f32[64,64]{1,0:T(8,128)S(1)} %bitcast.17, bf16[32,9,64,64]{3,2,1,0:T(8,128)(2,1)} %refs_2_.1, bf16[4,64,64]{2,1,0:T(8,128)(2,1)S(1)} %copy-done.1, f32[3]{0:T(128)S(1)} %copy-done.5, ...), custom_call_target="tpu_custom_call" | custom-call | tf_op jit(solution)/shard_map/pallas_call | solution.py:235
  45.4 0.5 %slice_bitcast_fusion = f32[16]{0:T(128)} fusion(f32[1,128]{1,0:T(1,128)S(1)} %get-tuple-element.8), kind=kLoop, calls=%fused_computation | loop fusion | bytes 128 | tf_op jit(solution)/shard_map/squeeze | solution.py:269
  45.9 0.8 %copy.16 = bf16[32,2,4096]{2,1,0:T(2,128)(2,1)} copy(bf16[32,2,4096]{2,1,0:T(2,128)(2,1)S(1)} %bitcast.15) | data formatting | bytes 1048576
  46.7 0.6 %copy.17 = f32[32,64]{1,0:T(8,128)} copy(f32[32,64]{1,0:T(8,128)S(1)} %get-tuple-element.13) | data formatting | bytes 16384
Async XLA Ops:
  0.6 1.0 %copy-start = (bf16[32,2,4096]{2,1,0:T(2,128)(2,1)S(1)}, bf16[32,2,4096]{2,1,0:T(2,128)(2,1)}, u32[]{:S(2)}) copy-start(bf16[32,2,4096]{2,1,0:T(2,128)(2,1)} %param.9) | copy-start | bytes 1572868
  1.7 0.8 %copy-start.1 = (bf16[4,64,64]{2,1,0:T(8,128)(2,1)S(1)}, bf16[4,64,64]{2,1,0:T(8,128)(2,1)}, u32[]{:S(2)}) copy-start(bf16[4,64,64]{2,1,0:T(8,128)(2,1)} %refs_3_.1) | copy-start | bytes 98308
  2.5 0.8 %copy-start.2 = (f32[32,2,64]{2,1,0:T(2,128)S(1)}, f32[32,2,64]{2,1,0:T(2,128)}, u32[]{:S(2)}) copy-start(f32[32,2,64]{2,1,0:T(2,128)} %param.11) | copy-start | bytes 49156
  3.3 0.7 %copy-start.3 = (s32[32,4]{0,1:T(4,128)S(1)}, s32[32,4]{0,1:T(4,128)}, u32[]{:S(2)}) copy-start(s32[32,4]{0,1:T(4,128)} %param.13) | copy-start | bytes 1540
  4.0 0.7 %copy-start.4 = (s32[32,4]{0,1:T(4,128)S(1)}, s32[32,4]{0,1:T(4,128)}, u32[]{:S(2)}) copy-start(s32[32,4]{0,1:T(4,128)} %param.14) | copy-start | bytes 1540
  4.6 0.7 %copy-start.5 = (f32[3]{0:T(128)S(1)}, f32[3]{0:T(128)}, u32[]{:S(2)}) copy-start(f32[3]{0:T(128)} %refs_4_.1) | copy-start | bytes 40
  5.3 0.7 %copy-start.6 = (f32[16]{0:T(128)S(1)}, f32[16]{0:T(128)}, u32[]{:S(2)}) copy-start(f32[16]{0:T(128)} %refs_7_.1) | copy-start | bytes 196
  6.0 0.7 %copy-start.7 = (s32[32]{0:T(128)S(1)}, s32[32]{0:T(128)}, u32[]{:S(2)}) copy-start(s32[32]{0:T(128)} %refs_8_.1) | copy-start | bytes 388
